TPU v7x, 32 devices: a whole 2x2x4 slice. The times are simulated.
32 devices in a mesh: gx: 4 (over z), gy: 2 (over y), gz: 4 (over x, core).
Axes of the slice: x: 2, y: 2, z: 4, core: 2. Of those that a mesh axis runs over, the one named last changes fastest.
Arguments:
- ref_pos: float32 [256, 3, 128], P(('gx', 'gy', 'gz')), may hold values from -0.1 to 256, as said below
- displace: float32 [256, 3, 128], P(('gx', 'gy', 'gz')), may hold values from -0.1 to 0.1
- velocity: float32 [256, 3, 128], P(('gx', 'gy', 'gz')), may hold values from -15 to 15
- acceleration: float32 [256, 3, 128], P(('gx', 'gy', 'gz')), may hold values from -6 to 6
- new_owner: int32 [256], P(('gx', 'gy', 'gz')), may hold values from 0 to 31, as said below
- ghost_ids: int32 [768], P(('gx', 'gy', 'gz')), may hold values from 0 to 255, as said below
- pair_blocks: int32 [2, 6912], P(None, ('gx', 'gy', 'gz')), may hold values from 0 to 31, as said below
- pair_count: int32 [32], P(('gx', 'gy', 'gz')), may hold values from 1 to 216, as said below
- bond_bits: int32 [6912, 12, 128], P(('gx', 'gy', 'gz')), may hold values from 0 to 2047, as said below
Outputs:
- displace_new: float32 [256, 3, 128], P(('gx', 'gy', 'gz'))
- velocity_new: float32 [256, 3, 128], P(('gx', 'gy', 'gz'))
- acceleration_new: float32 [256, 3, 128], P(('gx', 'gy', 'gz'))
Inputs may be any that keep to these rules, and one draw needn't show every extreme that they name: `new_owner`: each block's new owner is its own device or one of the 26 devices around it in the grid gx by gy by gz, wrapping around every axis; exactly 2 blocks of each device get another owner, and every device is the new owner of exactly 8 blocks. `ghost_ids`: block indices in the new layout; each names a block whose new owner is one of the 26 devices around the device of the list, wrapping around; a list may name a block more than once; a list names at most 3 entries whose blocks have the same owner, and exactly 3 for some owner in every list. `pair_blocks`: row 0 is a slot of the device (below 8); row 1 is an index into the device's 8 blocks followed by its 24 ghost blocks. `pair_count`: at least one device has all 216 slots live in every draw. `bond_bits`: bits of particles at 128 or beyond are not used. `ref_pos`: reference positions of two different particles are at least 0.65 apart.
All inputs are finite; a program needn't handle non-finite values. Where the computation divides by a largest or mean magnitude, that divisor is 1e-20 or more.
Results may differ from a plain program's by a relative error of at most 0.0003.
Values sent between devices are 32-bit elements; how exact they have to be, the bound alone decides.
A program may use at most 64 MiB of HBM per device.

v0:
```python
import functools

import jax
import jax.numpy as jnp
from jax import lax
from jax.experimental import pallas as pl
from jax.experimental.pallas import tpu as pltpu
from jax.sharding import PartitionSpec as P

WORD_BITS = 11


courant = 0.05
stiffness = 20.0


MESH = pl.DeviceIdType.MESH
AXES = ("gx", "gy", "gz")
MOVERS = 2
REQUESTS = 3
STATE = 12
SUBLANES = 8
OWNER_ROW = 1
GHOST_ROW = OWNER_ROW + MOVERS
CARD = GHOST_ROW + 1
UNROLLED = 64
TOGETHER = 2


def reach(size):
    return (0,) if size == 1 else (0, 1) if size == 2 else (-1, 0, 1)


def cell_rank(place, step, size):
    if size < 3:
        return (place + step) % size
    first = (size - place) // size
    last = (place + 1) // size
    return (step + 1 + 2 * first + last) % 3


def cell_of(places, steps, sizes):
    cell = 0
    for place, step, size in zip(places, steps, sizes):
        cell = cell * len(reach(size)) + cell_rank(place, step, size)
    return cell


def neighbour_steps(sizes):
    every = [(x, y, z) for x in reach(sizes[0]) for y in reach(sizes[1]) for z in reach(sizes[2])]
    return [steps for steps in every if steps != (0, 0, 0)]


def cell_target(places, ranks, sizes):
    target = []
    for place, rank, size in zip(places, ranks, sizes):
        if size < 3:
            target.append(jnp.int32(rank))
        else:
            first = (size - place) // size
            last = (place + 1) // size
            target.append((place + (rank + 6 - 2 * first - last) % 3 - 1 + size) % size)
    return target


def exchange_kernel(
    sizes,
    owner_ref, ghost_ref, ref_ref, disp_ref, vel_ref, acc_ref,
    local_ref, ghosts_ref, half_ref, step_ref,
    arrived_ref, card_ref, pack_ref, list_ref, ask_ref, flat_ref,
    send_sems, recv_sems,
):
    dims, blocks, particles = ref_ref.shape
    total = sizes[0] * sizes[1] * sizes[2]
    steps_all = neighbour_steps(sizes)
    cells = len(steps_all) + 1
    extents = [len(reach(size)) for size in sizes]
    ranks_all = [
        (x, y, z) for x in range(extents[0]) for y in range(extents[1]) for z in range(extents[2])
    ]
    places = [lax.axis_index(name) for name in AXES]
    myself = (places[0] * sizes[1] + places[1]) * sizes[2] + places[2]
    mine = cell_of(places, (0, 0, 0), sizes)
    sources = (ref_ref, disp_ref, vel_ref, acc_ref)

    def to_others(action):
        if total <= UNROLLED:
            coords = [
                [(place + step) % size for step in range(size)]
                for place, size in zip(places, sizes)
            ]
            for x in range(sizes[0]):
                for y in range(sizes[1]):
                    for z in range(sizes[2]):
                        if (x, y, z) != (0, 0, 0):
                            action((coords[0][x], coords[1][y], coords[2][z]))
        else:

            def act(number, carry):
                device = (myself + number) % total
                rest = device // sizes[2]
                action((rest // sizes[1], rest % sizes[1], device % sizes[2]))
                return carry

            lax.fori_loop(1, total, act, 0)

    barrier = pltpu.get_barrier_semaphore()
    to_others(
        lambda target: pl.semaphore_signal(barrier, inc=1, device_id=target, device_id_type=MESH)
    )

    leavers = [jnp.int32(0) for _ in range(MOVERS)]
    seen = jnp.int32(0)
    for block in range(blocks):
        leaves = jnp.where(owner_ref[block] != myself, 1, 0)
        for order in range(MOVERS):
            leavers[order] += block * leaves * jnp.where(seen == order, 1, 0)
        seen += leaves
    speeds = jnp.max(jnp.abs(vel_ref[...]), axis=0)
    card_ref[myself, pl.ds(0, 1), :] = jnp.max(speeds, axis=0, keepdims=True)
    for order in range(MOVERS):
        owner = jnp.full((1, particles), owner_ref[leavers[order]], jnp.int32)
        card_ref[myself, pl.ds(OWNER_ROW + order, 1), :] = owner.astype(jnp.float32)
    card_ref[myself, pl.ds(GHOST_ROW, 1), :] = ghost_ref[...]
    for order in range(MOVERS):
        for part, source in enumerate(sources):
            for dim in range(dims):
                row = order * STATE + part * dims + dim
                arrived_ref[mine, pl.ds(row, 1), :] = source[dim, pl.ds(leavers[order], 1), :]

    pl.semaphore_wait(barrier, total - 1)

    def send_card(target):
        pltpu.make_async_remote_copy(
            src_ref=card_ref.at[myself],
            dst_ref=card_ref.at[myself],
            send_sem=send_sems.at[0],
            recv_sem=recv_sems.at[0],
            device_id=target,
            device_id_type=MESH,
        ).start()

    def send_halo(steps, source_of, ref, kind):
        target = [(place + step) % size for place, step, size in zip(places, steps, sizes)]
        back = [-step for step in steps]
        pltpu.make_async_remote_copy(
            src_ref=source_of(cell_of(places, steps, sizes)),
            dst_ref=ref.at[cell_of(target, back, sizes)],
            send_sem=send_sems.at[kind],
            recv_sem=recv_sems.at[kind],
            device_id=tuple(target),
            device_id_type=MESH,
        ).start()

    def all_bytes(ref, sem):
        part = ref.at[pl.ds(0, ref.shape[0] - 1)]
        return pltpu.make_async_copy(part, part, sem)

    to_others(send_card)
    for steps in steps_all:
        send_halo(steps, lambda cell: arrived_ref.at[mine], arrived_ref, 1)

    all_bytes(card_ref, recv_sems.at[0]).wait()
    fastest = jnp.max(jnp.max(card_ref[:, pl.ds(0, 1), :], axis=0), axis=1, keepdims=True)
    timestep = jnp.broadcast_to(courant / (fastest + 1e-06), (blocks, particles))
    step_ref[...] = timestep

    name = myself.astype(jnp.float32)
    slot = lax.broadcasted_iota(jnp.int32, (blocks, particles), 0).astype(jnp.float32)
    count = jnp.zeros((1, particles), jnp.float32)
    own_start = jnp.zeros((1, particles), jnp.float32)
    goals = []
    list_ref[...] = jnp.zeros_like(list_ref)
    for cell, ranks in enumerate(ranks_all):
        target = cell_target(places, ranks, sizes)
        device = (target[0] * sizes[1] + target[1]) * sizes[2] + target[2]
        list_ref[pl.ds(cell, 1), :] = card_ref[device, pl.ds(GHOST_ROW, 1), :]
        own = jnp.where(mine == cell, 1.0, 0.0)
        own_start = own_start + own * count
        count = count + own * (blocks - MOVERS)
        for order in range(MOVERS):
            hit = card_ref[device, pl.ds(OWNER_ROW + order, 1), :] == name
            goals.append(jnp.where(hit, count, -1.0))
            count = count + jnp.where(hit, 1.0, 0.0)

    ids = list_ref[...]
    owners = jnp.floor((ids + 0.5) * (1.0 / blocks))
    wanted = owners == name
    lane_from = lax.broadcasted_iota(jnp.int32, (particles, particles), 0)
    lane_to = lax.broadcasted_iota(jnp.int32, (particles, particles), 1)
    earlier = jnp.where(lane_from < lane_to, 1.0, 0.0)
    ranked = jnp.dot(
        jnp.where(wanted, 1.0, 0.0), earlier, preferred_element_type=jnp.float32
    )
    for request in range(REQUESTS):
        fits = jnp.logical_and(wanted, jnp.abs(ranked - request) < 0.5)
        slots = jnp.sum(jnp.where(fits, ids - owners * blocks, 0.0), axis=1, keepdims=True)
        ask_ref[request] = jnp.broadcast_to(slots, ids.shape)

    all_bytes(arrived_ref, recv_sems.at[1]).wait()
    settled = [jnp.zeros((blocks, particles), jnp.float32) for _ in range(STATE)]
    for cell in range(cells):
        for order in range(MOVERS):
            chosen = slot == goals[cell * MOVERS + order]
            for comp in range(STATE):
                row = arrived_ref[cell, pl.ds(order * STATE + comp, 1), :]
                settled[comp] = jnp.where(chosen, row, settled[comp])
    stayed = jnp.int32(0)
    for block in range(blocks):
        stays = jnp.where(owner_ref[block] == myself, 1, 0)
        offset = jnp.where(stays == 1, stayed, -2 * blocks * MOVERS * cells).astype(jnp.float32)
        chosen = slot == own_start + offset
        for part, source in enumerate(sources):
            for dim in range(dims):
                comp = part * dims + dim
                row = source[dim, pl.ds(block, 1), :]
                settled[comp] = jnp.where(chosen, row, settled[comp])
        stayed += stays

    for dim in range(dims):
        halfway = settled[2 * dims + dim] + 0.5 * timestep * settled[3 * dims + dim]
        half_ref[dim] = halfway
        flat_ref[pl.ds(dim * blocks, blocks), :] = settled[dim]
        flat_ref[pl.ds((dims + dim) * blocks, blocks), :] = settled[dims + dim] + timestep * halfway
    comps = 2 * dims
    blocks_rows = []
    for block in range(blocks):
        rows = flat_ref[pl.ds(block, comps, stride=blocks), :]
        local_ref[block] = rows
        blocks_rows.append(rows)
    for cell in range(cells):
        for request in range(REQUESTS):
            ask = jnp.broadcast_to(ask_ref[request, pl.ds(cell, 1), :], (comps, particles))
            picked = blocks_rows[0]
            for block in range(1, blocks):
                picked = jnp.where(ask == block, blocks_rows[block], picked)
            pack_ref[cell, request] = picked

    for steps in steps_all:
        send_halo(steps, lambda cell: pack_ref.at[cell], ghosts_ref, 2)
    all_bytes(ghosts_ref, recv_sems.at[2]).wait()
    all_bytes(card_ref, send_sems.at[0]).wait()
    all_bytes(arrived_ref, send_sems.at[1]).wait()
    all_bytes(ghosts_ref, send_sems.at[2]).wait()


def exchange(sizes, new_owner, ghost_ids, ref_pos, displace, velocity, acceleration):
    dims, blocks, particles = ref_pos.shape
    cells = len(neighbour_steps(sizes)) + 1
    total = sizes[0] * sizes[1] * sizes[2]
    padded = -(-cells // SUBLANES) * SUBLANES
    ghosts = ghost_ids.astype(jnp.float32)[None]
    ghosts = jnp.pad(ghosts, ((0, 0), (0, particles - ghosts.shape[1])), constant_values=-blocks)
    smem = pl.BlockSpec(memory_space=pltpu.SMEM)
    vmem = pl.BlockSpec(memory_space=pltpu.VMEM)
    return pl.pallas_call(
        functools.partial(exchange_kernel, sizes),
        out_shape=(
            jax.ShapeDtypeStruct((blocks, 2 * dims, particles), jnp.float32),
            jax.ShapeDtypeStruct((cells, REQUESTS, 2 * dims, particles), jnp.float32),
            jax.ShapeDtypeStruct((dims, blocks, particles), jnp.float32),
            jax.ShapeDtypeStruct((blocks, particles), jnp.float32),
        ),
        in_specs=[smem, vmem, vmem, vmem, vmem, vmem],
        out_specs=(vmem, vmem, vmem, vmem),
        scratch_shapes=[
            pltpu.VMEM((cells, MOVERS * STATE, particles), jnp.float32),
            pltpu.VMEM((total, CARD, particles), jnp.float32),
            pltpu.VMEM((cells, REQUESTS, 2 * dims, particles), jnp.float32),
            pltpu.VMEM((padded, particles), jnp.float32),
            pltpu.VMEM((REQUESTS, padded, particles), jnp.float32),
            pltpu.VMEM((2 * dims * blocks, particles), jnp.float32),
            pltpu.SemaphoreType.DMA((3,)),
            pltpu.SemaphoreType.DMA((3,)),
        ],
        compiler_params=pltpu.CompilerParams(
            collective_id=0, has_side_effects=True, vmem_limit_bytes=16 * 1024 * 1024
        ),
    )(new_owner, ghosts, ref_pos, displace, velocity, acceleration)


def spread_away(index_ref, local_ref, ghosts_ref, rows_ref, turned_ref, order_ref, wide_ref):
    extended, comps, particles = rows_ref.shape
    blocks = local_ref.shape[0]
    batch = particles // comps
    used = local_ref.shape[1]
    aligned = SUBLANES * WORD_BITS
    groups = particles // SUBLANES
    rows_ref[...] = jnp.zeros_like(rows_ref)
    for block in range(blocks):
        rows_ref[block, pl.ds(0, used), :] = local_ref[block]
    for ghost in range(extended - blocks):
        rows_ref[blocks + ghost, pl.ds(0, used), :] = ghosts_ref[index_ref[ghost]]
    for part in range(extended // batch):
        rows = rows_ref[pl.ds(part * batch, batch)].reshape(particles, particles)
        turned_ref[...] = rows.T
        for step in range(groups):
            if step < WORD_BITS:
                column = turned_ref[pl.ds(step, SUBLANES, stride=WORD_BITS), :]
            else:
                start = aligned + (step - WORD_BITS) * SUBLANES
                column = turned_ref[pl.ds(start, SUBLANES), :]
            order_ref[part * groups + step] = column

    def spread_step(number, carry):
        part, step = number // groups, number % groups
        column = order_ref[number]
        for block in range(batch):
            for comp in range(used):
                place = block * comps + comp
                wide_ref[part * batch + block, step, comp] = jnp.broadcast_to(
                    column[:, place : place + 1], (SUBLANES, particles)
                )
        return carry

    lax.fori_loop(0, extended // batch * groups, spread_step, 0)


def tail_steps(particles):
    starts = range(SUBLANES * WORD_BITS, particles, SUBLANES)
    return [(start, start // WORD_BITS, (start + SUBLANES - 1) // WORD_BITS) for start in starts]


def tile_sum(home, away, front, back, wide_ref, bit_ref, particles):
    sublane = lax.broadcasted_iota(jnp.int32, (SUBLANES, particles), 0)
    sums = [jnp.zeros((SUBLANES, particles), jnp.float32) for _ in range(3)]
    tails = tail_steps(particles)
    for step in range(particles // SUBLANES):
        if step < WORD_BITS:
            hit = jnp.bitwise_and(front, 1 << step)
        else:
            start, low, high = tails[step - WORD_BITS]
            low, high = low - SUBLANES, high - SUBLANES
            row = jnp.broadcast_to(back[low : low + 1], (SUBLANES, particles))
            if high != low:
                upper = jnp.broadcast_to(back[high : high + 1], (SUBLANES, particles))
                row = jnp.where(sublane < (high + SUBLANES) * WORD_BITS - start, row, upper)
            hit = jnp.bitwise_and(row, bit_ref[step - WORD_BITS])
        other = [wide_ref[away, step, comp] for comp in range(6)]
        ref_gap = [other[k] - home[k] for k in range(3)]
        now_gap = [ref_gap[k] + (other[3 + k] - home[3 + k]) for k in range(3)]
        ref_sq = ref_gap[0] * ref_gap[0] + ref_gap[1] * ref_gap[1] + ref_gap[2] * ref_gap[2]
        now_sq = now_gap[0] * now_gap[0] + now_gap[1] * now_gap[1] + now_gap[2] * now_gap[2]
        scaled = jnp.where(hit != 0, lax.rsqrt(ref_sq) - lax.rsqrt(now_sq), 0.0)
        sums = [sums[k] + scaled * now_gap[k] for k in range(3)]
    return sums


def bond_kernel(
    words, pairs_ref, count_ref, index_ref, local_ref, ghosts_ref, half_ref, step_ref, bits_ref,
    displace_ref, velocity_ref, accel_ref,
    rows_ref, turned_ref, order_ref, wide_ref, total_ref, bit_ref,
):
    _, blocks, particles = accel_ref.shape
    pairs = bits_ref.shape[0] // words
    spread_away(index_ref, local_ref, ghosts_ref, rows_ref, turned_ref, order_ref, wide_ref)
    total_ref[...] = jnp.zeros_like(total_ref)
    sublane = lax.broadcasted_iota(jnp.int32, (SUBLANES, particles), 0)
    for number, (start, _, _) in enumerate(tail_steps(particles)):
        bit_ref[number] = jnp.left_shift(1, (sublane + start) % WORD_BITS)

    def not_own(first, rows):
        word = lax.broadcasted_iota(jnp.int32, (rows, particles), 0) + first
        lane = lax.broadcasted_iota(jnp.int32, (rows, particles), 1)
        own = jnp.where(lane // WORD_BITS == word, jnp.left_shift(1, lane % WORD_BITS), 0)
        return jnp.bitwise_not(own)

    behind = words - SUBLANES
    keep_front, keep_back = not_own(0, SUBLANES), not_own(SUBLANES, behind)
    count = count_ref[0]

    def pair_sums(wish):
        slot = jnp.minimum(wish, pairs - 1)
        live = jnp.where(wish < count, -1, 0)
        home_id = pairs_ref[0, slot]
        away_id = pairs_ref[1, slot]
        home = [
            jnp.broadcast_to(rows_ref[home_id, pl.ds(comp, 1), :], (SUBLANES, particles))
            for comp in range(6)
        ]
        apart = jnp.where(home_id == away_id, 0, -1)
        front = bits_ref[pl.ds(slot, SUBLANES, stride=pairs), :]
        back = bits_ref[pl.ds(slot + SUBLANES * pairs, behind, stride=pairs), :]
        front = front & ((keep_front | apart) & live)
        back = back & ((keep_back | apart) & live)
        return home_id, tile_sum(home, away_id, front, back, wide_ref, bit_ref, particles)

    def add_pairs(number, carry):
        found = [pair_sums(number * TOGETHER + order) for order in range(TOGETHER)]
        for home_id, sums in found:
            for comp in range(3):
                total_ref[home_id, comp] += sums[comp]
        return carry

    lax.fori_loop(0, (count + TOGETHER - 1) // TOGETHER, add_pairs, 0)
    accel = stiffness * jnp.sum(total_ref[...], axis=2)
    for comp in range(3):
        for block in range(blocks):
            accel_ref[comp, pl.ds(block, 1), :] = accel[block, comp : comp + 1]
            displace_ref[comp, pl.ds(block, 1), :] = local_ref[block, pl.ds(3 + comp, 1), :]
        velocity_ref[comp] = half_ref[comp] + 0.5 * step_ref[...] * accel_ref[comp]


def bond_step(index, local, ghosts, half, step, pair_blocks, pair_count, bond_bits):
    blocks, particles = step.shape
    extended = index.shape[0] + blocks
    words, pairs = bond_bits.shape[0:2]
    shape = jax.ShapeDtypeStruct((3, blocks, particles), jnp.float32)
    smem = pl.BlockSpec(memory_space=pltpu.SMEM)
    vmem = pl.BlockSpec(memory_space=pltpu.VMEM)
    groups = particles // SUBLANES
    return pl.pallas_call(
        functools.partial(bond_kernel, words),
        out_shape=(shape, shape, shape),
        in_specs=[smem, smem, smem, vmem, vmem, vmem, vmem, vmem],
        out_specs=(vmem, vmem, vmem),
        scratch_shapes=[
            pltpu.VMEM((extended, SUBLANES, particles), jnp.float32),
            pltpu.VMEM((particles, particles), jnp.float32),
            pltpu.VMEM((extended * SUBLANES // particles * groups, SUBLANES, particles), jnp.float32),
            pltpu.VMEM((extended, groups, 6, SUBLANES, particles), jnp.float32),
            pltpu.VMEM((blocks, 3, SUBLANES, particles), jnp.float32),
            pltpu.VMEM((len(tail_steps(particles)), SUBLANES, particles), jnp.int32),
        ],
        compiler_params=pltpu.CompilerParams(vmem_limit_bytes=40 * 1024 * 1024),
    )(pair_blocks, pair_count, index, local, ghosts, half, step, bond_bits.reshape(words * pairs, particles))


def per_device(
    ref_pos,
    displace,
    velocity,
    acceleration,
    new_owner,
    ghost_ids,
    pair_blocks,
    pair_count,
    bond_bits,
):
    blocks = ref_pos.shape[0]
    sizes = tuple(lax.axis_size(name) for name in AXES)
    places = [lax.axis_index(name) for name in AXES]
    turned = [array.transpose(1, 0, 2) for array in (ref_pos, displace, velocity, acceleration)]
    local, ghosts, half, step = exchange(sizes, new_owner, ghost_ids, *turned)
    ghost_dev = ghost_ids // blocks
    ghost_places = (
        ghost_dev // (sizes[1] * sizes[2]),
        ghost_dev // sizes[2] % sizes[1],
        ghost_dev % sizes[2],
    )
    moves = []
    for ghost, place, size in zip(ghost_places, places, sizes):
        apart = (ghost - place) % size
        moves.append(jnp.where(apart == size - 1, -1, apart) if size > 2 else apart)
    ghost_cell = cell_of(places, moves, sizes)
    order = jnp.arange(ghost_ids.shape[0])
    repeats = (ghost_dev[:, None] == ghost_dev[None, :]) & (order[None, :] < order[:, None])
    index = ghost_cell * REQUESTS + jnp.sum(repeats.astype(jnp.int32), axis=1)
    ghosts = ghosts.reshape((-1,) + ghosts.shape[2:])
    results = bond_step(
        index, local, ghosts, half, step, pair_blocks, pair_count, bond_bits.transpose(1, 0, 2)
    )
    return tuple(array.transpose(1, 0, 2) for array in results)


def solution(mesh):
    in_specs = (
        P(("gx", "gy", "gz"), None, None),
        P(("gx", "gy", "gz"), None, None),
        P(("gx", "gy", "gz"), None, None),
        P(("gx", "gy", "gz"), None, None),
        P(("gx", "gy", "gz")),
        P(("gx", "gy", "gz")),
        P(None, ("gx", "gy", "gz")),
        P(("gx", "gy", "gz")),
        P(("gx", "gy", "gz"), None, None),
    )
    out_specs = (
        P(("gx", "gy", "gz"), None, None),
        P(("gx", "gy", "gz"), None, None),
        P(("gx", "gy", "gz"), None, None),
    )
    return jax.shard_map(
        per_device, mesh=mesh, in_specs=in_specs, out_specs=out_specs, check_vma=False
    )
```

profile of v0, /device:TPU:16, one launch (start us, length us, event | category | flops | bytes accessed | tf_op | source)
XLA Modules:
  0.0 50.2 jit_solution(696536643574081066)
XLA Ops:
  1.3 0.7 %convert_bitcast_fusion = (f32[1,24]{1,0:T(1,128)S(1)}, s32[24]{0:T(128)S(1)}) fusion(s32[24]{0:T(128)} %param.14), kind=kLoop, calls=%fused_computation.53 | loop fusion | flops 384 | bytes 288 | tf_op jit(solution)/shard_map/broadcast_in_dim | solution.py:252
  2.0 0.2 convert_reduce_fusion
  2.3 0.0 copy-start.1
  2.3 0.7 %copy-done.1 = f32[8,3,128]{2,0,1:T(8,128)S(1)} copy-done((f32[8,3,128]{2,0,1:T(8,128)S(1)}, f32[8,3,128]{2,0,1:T(8,128)}, u32[]{:S(2)}) %copy-start.1) | copy-done | bytes 12312
  3.0 0.0 copy-start.2
  3.0 0.7 %copy-done.2 = f32[8,3,128]{2,0,1:T(8,128)S(1)} copy-done((f32[8,3,128]{2,0,1:T(8,128)S(1)}, f32[8,3,128]{2,0,1:T(8,128)}, u32[]{:S(2)}) %copy-start.2) | copy-done | bytes 12312
  3.7 0.0 copy-start.3
  3.7 0.7 %copy-done.3 = f32[8,3,128]{2,0,1:T(8,128)S(1)} copy-done((f32[8,3,128]{2,0,1:T(8,128)S(1)}, f32[8,3,128]{2,0,1:T(8,128)}, u32[]{:S(2)}) %copy-start.3) | copy-done | bytes 12312
  4.4 0.0 copy-start.4
  4.4 0.7 %copy-done.4 = f32[8,3,128]{2,0,1:T(8,128)S(1)} copy-done((f32[8,3,128]{2,0,1:T(8,128)S(1)}, f32[8,3,128]{2,0,1:T(8,128)}, u32[]{:S(2)}) %copy-start.4) | copy-done | bytes 12312
  5.1 0.0 copy-start.6
  5.1 0.7 %copy-done.6 = s32[8]{0:T(128)S(1)} copy-done((s32[8]{0:T(128)S(1)}, s32[8]{0:T(128)}, u32[]{:S(2)}) %copy-start.6) | copy-done | bytes 56
  5.7 17.1 %shard_map.112 = (f32[8,6,128]{2,1,0:T(8,128)S(1)}, f32[18,3,6,128]{3,2,1,0:T(8,128)S(1)}, f32[3,8,128]{2,1,0:T(8,128)S(1)}, f32[8,128]{1,0:T(8,128)S(1)}) custom-call(s32[8]{0:T(128)S(1)} %copy-done.6, f32[1,128]{1,0:T(1,128)S(1)} %pad.4.ghost_ref, f32[3,8,128]{2,1,0:T(8,128)S(1)} %bitcast.15, f32[3,8,128]{2,1,0:T(8,128)S(1)} %bitcast.16, ...), custom_call_target="tpu_custom_call" | custom-call | tf_op jit(solution)/shard_map/pallas_call | solution.py:256
  22.9 0.0 copy-start
  22.9 1.3 %copy-done = s32[216,12,128]{2,0,1:T(8,128)S(1)} copy-done((s32[216,12,128]{2,0,1:T(8,128)S(1)}, s32[216,12,128]{2,0,1:T(8,128)}, u32[]{:S(2)}) %copy-start) | copy-done | bytes 1327128
  24.2 0.0 copy-start.5
  24.2 0.7 %copy-done.5 = s32[2,216]{1,0:T(2,128)S(1)} copy-done((s32[2,216]{1,0:T(2,128)S(1)}, s32[2,216]{1,0:T(2,128)}, u32[]{:S(2)}) %copy-start.5) | copy-done | bytes 1752
  24.9 25.3 %shard_map.113 = (f32[3,8,128]{2,1,0:T(8,128)}, f32[3,8,128]{2,1,0:T(8,128)}, f32[3,8,128]{2,1,0:T(8,128)}) custom-call(s32[2,216]{1,0:T(2,128)S(1)} %copy-done.5, s32[1]{0:T(128)S(6)} %copy.12.count_ref, s32[24]{0:T(128)S(1)} %multiply_add_fusion.index_ref, f32[8,6,128]{2,1,0:T(8,128)S(1)} %get-tuple-element.10.local_ref, f32[54,6,128]{2,1,0:T(8,128)S(1)} %bitcast.14, ...), custom_call_target="tpu_custom_call" | custom-call | tf_op jit(solution)/shard_map/pallas_call | solution.py:412
  (2 shorter events, 0.0 us)
Async XLA Ops:
  2.3 0.7 %copy-start.1 = (f32[8,3,128]{2,0,1:T(8,128)S(1)}, f32[8,3,128]{2,0,1:T(8,128)}, u32[]{:S(2)}) copy-start(f32[8,3,128]{2,0,1:T(8,128)} %param.9) | copy-start | bytes 36868
  3.0 0.7 %copy-start.2 = (f32[8,3,128]{2,0,1:T(8,128)S(1)}, f32[8,3,128]{2,0,1:T(8,128)}, u32[]{:S(2)}) copy-start(f32[8,3,128]{2,0,1:T(8,128)} %param.10) | copy-start | bytes 36868
  3.7 0.7 %copy-start.3 = (f32[8,3,128]{2,0,1:T(8,128)S(1)}, f32[8,3,128]{2,0,1:T(8,128)}, u32[]{:S(2)}) copy-start(f32[8,3,128]{2,0,1:T(8,128)} %param.11) | copy-start | bytes 36868
  4.4 0.7 %copy-start.4 = (f32[8,3,128]{2,0,1:T(8,128)S(1)}, f32[8,3,128]{2,0,1:T(8,128)}, u32[]{:S(2)}) copy-start(f32[8,3,128]{2,0,1:T(8,128)} %param.12) | copy-start | bytes 36868
  5.1 0.7 %copy-start.6 = (s32[8]{0:T(128)S(1)}, s32[8]{0:T(128)}, u32[]{:S(2)}) copy-start(s32[8]{0:T(128)} %owner_ref.1) | copy-start | bytes 100
  22.9 1.3 %copy-start = (s32[216,12,128]{2,0,1:T(8,128)S(1)}, s32[216,12,128]{2,0,1:T(8,128)}, u32[]{:S(2)}) copy-start(s32[216,12,128]{2,0,1:T(8,128)} %param.17) | copy-start | bytes 3981316
  24.2 0.7 %copy-start.5 = (s32[2,216]{1,0:T(2,128)S(1)}, s32[2,216]{1,0:T(2,128)}, u32[]{:S(2)}) copy-start(s32[2,216]{1,0:T(2,128)} %pairs_ref.1) | copy-start | bytes 5188
where the time goes:
time: 50.7 us; the launch traced here: 50.2 us
  Pallas kernels  42.5 us (84%)
  local copies, waits for them, and re-layouts  5.48 us (11%)
  between operations  1.33 us (3%)
  other arithmetic  0.96 us (2%)
    pallas_call x1, Pallas kernels, bond_step(): pl.pallas_call(functools.partial(bond_kernel, words), out_shape=(shape, s...  25.3 us
    pallas_call x1, Pallas kernels, exchange(): pl.pallas_call(functools.partial(exchange_kernel, sizes), out_shape=(jax....  17.1 us
    unnamed x14, local copies, waits for them, and re-layouts  5.47 us

commit v1 on v0

--- a/solution.py
+++ b/solution.py
@@ -65,12 +65,21 @@
 
 def exchange_kernel(
     sizes,
+    owner_in, ghost_in, ref_in, disp_in, vel_in, acc_in,
+    ext_ref, half_ref, step_ref,
     owner_ref, ghost_ref, ref_ref, disp_ref, vel_ref, acc_ref,
-    local_ref, ghosts_ref, half_ref, step_ref,
-    arrived_ref, card_ref, pack_ref, list_ref, ask_ref, flat_ref,
-    send_sems, recv_sems,
+    arrived_ref, card_ref, pack_ref, ghosts_ref, list_ref, ask_ref, flat_ref,
+    send_sems, recv_sems, load_sems,
 ):
     dims, blocks, particles = ref_ref.shape
+    inner = (owner_ref, ghost_ref, ref_ref, disp_ref, vel_ref, acc_ref)
+    outer = (owner_in, ghost_in, ref_in, disp_in, vel_in, acc_in)
+    loads = [
+        pltpu.make_async_copy(source, target, load_sems.at[number])
+        for number, (source, target) in enumerate(zip(outer, inner))
+    ]
+    for load in loads:
+        load.start()
     total = sizes[0] * sizes[1] * sizes[2]
     steps_all = neighbour_steps(sizes)
     cells = len(steps_all) + 1
@@ -109,6 +118,8 @@
         lambda target: pl.semaphore_signal(barrier, inc=1, device_id=target, device_id_type=MESH)
     )
 
+    for load in loads:
+        load.wait()
     leavers = [jnp.int32(0) for _ in range(MOVERS)]
     seen = jnp.int32(0)
     for block in range(blocks):
@@ -121,7 +132,12 @@
     for order in range(MOVERS):
         owner = jnp.full((1, particles), owner_ref[leavers[order]], jnp.int32)
         card_ref[myself, pl.ds(OWNER_ROW + order, 1), :] = owner.astype(jnp.float32)
-    card_ref[myself, pl.ds(GHOST_ROW, 1), :] = ghost_ref[...]
+    ghosts = ghost_ref.shape[0]
+    lane = lax.broadcasted_iota(jnp.int32, (1, particles), 1)
+    wish = jnp.full((1, particles), -blocks, jnp.int32)
+    for ghost in range(ghosts):
+        wish = jnp.where(lane == ghost, ghost_ref[ghost], wish)
+    card_ref[myself, pl.ds(GHOST_ROW, 1), :] = wish.astype(jnp.float32)
     for order in range(MOVERS):
         for part, source in enumerate(sources):
             for dim in range(dims):
@@ -226,7 +242,8 @@
     blocks_rows = []
     for block in range(blocks):
         rows = flat_ref[pl.ds(block, comps, stride=blocks), :]
-        local_ref[block] = rows
+        ext_ref[block] = jnp.zeros((SUBLANES, particles), jnp.float32)
+        ext_ref[block, pl.ds(0, comps), :] = rows
         blocks_rows.append(rows)
     for cell in range(cells):
         for request in range(REQUESTS):
@@ -238,7 +255,25 @@
 
     for steps in steps_all:
         send_halo(steps, lambda cell: pack_ref.at[cell], ghosts_ref, 2)
+    taken = []
+    for ghost in range(ghosts):
+        device = lax.div(ghost_ref[ghost], blocks)
+        rest = lax.div(device, sizes[2])
+        spots = (lax.div(rest, sizes[1]), lax.rem(rest, sizes[1]), lax.rem(device, sizes[2]))
+        moves = []
+        for spot, place, size in zip(spots, places, sizes):
+            apart = lax.rem(spot - place + size, size)
+            moves.append(jnp.where(apart == size - 1, -1, apart) if size > 2 else apart)
+        repeats = jnp.int32(0)
+        for _, before in taken:
+            repeats += jnp.where(before == device, 1, 0)
+        taken.append((cell_of(places, moves, sizes) * REQUESTS + repeats, device))
+    for ghost in range(ghosts):
+        ext_ref[blocks + ghost] = jnp.zeros((SUBLANES, particles), jnp.float32)
     all_bytes(ghosts_ref, recv_sems.at[2]).wait()
+    for ghost, (index, _) in enumerate(taken):
+        rows = ghosts_ref[lax.div(index, REQUESTS), lax.rem(index, REQUESTS)]
+        ext_ref[blocks + ghost, pl.ds(0, comps), :] = rows
     all_bytes(card_ref, send_sems.at[0]).wait()
     all_bytes(arrived_ref, send_sems.at[1]).wait()
     all_bytes(ghosts_ref, send_sems.at[2]).wait()
@@ -249,71 +284,97 @@
     cells = len(neighbour_steps(sizes)) + 1
     total = sizes[0] * sizes[1] * sizes[2]
     padded = -(-cells // SUBLANES) * SUBLANES
-    ghosts = ghost_ids.astype(jnp.float32)[None]
-    ghosts = jnp.pad(ghosts, ((0, 0), (0, particles - ghosts.shape[1])), constant_values=-blocks)
-    smem = pl.BlockSpec(memory_space=pltpu.SMEM)
+    ghosts = ghost_ids.shape[0]
+    hbm = pl.BlockSpec(memory_space=pltpu.HBM)
     vmem = pl.BlockSpec(memory_space=pltpu.VMEM)
     return pl.pallas_call(
         functools.partial(exchange_kernel, sizes),
         out_shape=(
-            jax.ShapeDtypeStruct((blocks, 2 * dims, particles), jnp.float32),
-            jax.ShapeDtypeStruct((cells, REQUESTS, 2 * dims, particles), jnp.float32),
+            jax.ShapeDtypeStruct((blocks + ghosts, SUBLANES, particles), jnp.float32),
             jax.ShapeDtypeStruct((dims, blocks, particles), jnp.float32),
             jax.ShapeDtypeStruct((blocks, particles), jnp.float32),
         ),
-        in_specs=[smem, vmem, vmem, vmem, vmem, vmem],
-        out_specs=(vmem, vmem, vmem, vmem),
+        in_specs=[hbm] * 6,
+        out_specs=(vmem, vmem, vmem),
         scratch_shapes=[
+            pltpu.SMEM(new_owner.shape, jnp.int32),
+            pltpu.SMEM(ghost_ids.shape, jnp.int32),
+            pltpu.VMEM(ref_pos.shape, jnp.float32),
+            pltpu.VMEM(ref_pos.shape, jnp.float32),
+            pltpu.VMEM(ref_pos.shape, jnp.float32),
+            pltpu.VMEM(ref_pos.shape, jnp.float32),
             pltpu.VMEM((cells, MOVERS * STATE, particles), jnp.float32),
             pltpu.VMEM((total, CARD, particles), jnp.float32),
+            pltpu.VMEM((cells, REQUESTS, 2 * dims, particles), jnp.float32),
             pltpu.VMEM((cells, REQUESTS, 2 * dims, particles), jnp.float32),
             pltpu.VMEM((padded, particles), jnp.float32),
             pltpu.VMEM((REQUESTS, padded, particles), jnp.float32),
             pltpu.VMEM((2 * dims * blocks, particles), jnp.float32),
             pltpu.SemaphoreType.DMA((3,)),
             pltpu.SemaphoreType.DMA((3,)),
+            pltpu.SemaphoreType.DMA((6,)),
         ],
         compiler_params=pltpu.CompilerParams(
             collective_id=0, has_side_effects=True, vmem_limit_bytes=16 * 1024 * 1024
         ),
-    )(new_owner, ghosts, ref_pos, displace, velocity, acceleration)
-
-
-def spread_away(index_ref, local_ref, ghosts_ref, rows_ref, turned_ref, order_ref, wide_ref):
-    extended, comps, particles = rows_ref.shape
-    blocks = local_ref.shape[0]
-    batch = particles // comps
-    used = local_ref.shape[1]
+    )(new_owner, ghost_ids, ref_pos, displace, velocity, acceleration)
+
+
+def spread_away(ext_ref, rows_ref, turned_ref, sorted_ref, mask_ref, ones_ref, wide_ref):
+    extended, comps, particles = ext_ref.shape
+    used = wide_ref.shape[1]
+    groups = wide_ref.shape[2]
+    halves = sorted_ref.shape[0]
+    stride = 4 * comps
+    batch = particles // stride
     aligned = SUBLANES * WORD_BITS
-    groups = particles // SUBLANES
     rows_ref[...] = jnp.zeros_like(rows_ref)
-    for block in range(blocks):
-        rows_ref[block, pl.ds(0, used), :] = local_ref[block]
-    for ghost in range(extended - blocks):
-        rows_ref[blocks + ghost, pl.ds(0, used), :] = ghosts_ref[index_ref[ghost]]
-    for part in range(extended // batch):
-        rows = rows_ref[pl.ds(part * batch, batch)].reshape(particles, particles)
-        turned_ref[...] = rows.T
-        for step in range(groups):
-            if step < WORD_BITS:
-                column = turned_ref[pl.ds(step, SUBLANES, stride=WORD_BITS), :]
-            else:
-                start = aligned + (step - WORD_BITS) * SUBLANES
-                column = turned_ref[pl.ds(start, SUBLANES), :]
-            order_ref[part * groups + step] = column
-
-    def spread_step(number, carry):
-        part, step = number // groups, number % groups
-        column = order_ref[number]
+    for block in range(extended):
+        rest = ext_ref[block]
+        for term in range(3):
+            part = rest.astype(jnp.bfloat16).astype(jnp.float32)
+            rows_ref[pl.ds(block * stride + term * comps, comps), :] = part
+            rest = rest - part
+    for number in range(2 * halves):
+        turned_ref[number] = rows_ref[pl.ds(number * particles, particles), :].T
+    for number in range(2 * halves):
+        half, column = number % halves, number // halves * particles
+        for pair in range(groups // 2):
+            parts = []
+            for step in (2 * pair, 2 * pair + 1):
+                if step < WORD_BITS:
+                    parts.append(turned_ref[number, pl.ds(step, SUBLANES, stride=WORD_BITS), :])
+                else:
+                    start = aligned + (step - WORD_BITS) * SUBLANES
+                    parts.append(turned_ref[number, pl.ds(start, SUBLANES), :])
+            both = jnp.concatenate(parts, axis=0).astype(jnp.bfloat16)
+            sorted_ref[half, pair, :, pl.ds(column, particles)] = both
+    lane = lax.broadcasted_iota(jnp.int32, mask_ref.shape[2:], 1) % particles
+    for block in range(batch):
+        for comp in range(used):
+            keep = jnp.logical_and(lane // stride == block, lane % comps == comp)
+            mask_ref[block, comp] = jnp.where(keep, 1.0, 0.0).astype(jnp.bfloat16)
+    above = lax.broadcasted_iota(jnp.int32, ones_ref.shape, 0) // particles
+    beside = lax.broadcasted_iota(jnp.int32, ones_ref.shape, 1) // particles
+    ones_ref[...] = jnp.where(above == beside, 1.0, 0.0).astype(jnp.bfloat16)
+
+    def spread_half(half, carry):
+        table = sorted_ref[half]
         for block in range(batch):
-            for comp in range(used):
-                place = block * comps + comp
-                wide_ref[part * batch + block, step, comp] = jnp.broadcast_to(
-                    column[:, place : place + 1], (SUBLANES, particles)
-                )
+            kept = [
+                (table * mask_ref[block, comp][None]).reshape(particles, 2 * particles)
+                for comp in range(used)
+            ]
+            spread = jnp.dot(
+                jnp.concatenate(kept, axis=0), ones_ref[...], preferred_element_type=jnp.float32
+            )
+            for side in range(2):
+                part = spread[:, side * particles : (side + 1) * particles]
+                place = (half + side * halves) * batch + block
+                wide_ref[place] = part.reshape(used, groups, SUBLANES, particles)
         return carry
 
-    lax.fori_loop(0, extended // batch * groups, spread_step, 0)
+    lax.fori_loop(0, halves, spread_half, 0)
 
 
 def tail_steps(particles):
@@ -336,7 +397,7 @@
                 upper = jnp.broadcast_to(back[high : high + 1], (SUBLANES, particles))
                 row = jnp.where(sublane < (high + SUBLANES) * WORD_BITS - start, row, upper)
             hit = jnp.bitwise_and(row, bit_ref[step - WORD_BITS])
-        other = [wide_ref[away, step, comp] for comp in range(6)]
+        other = [wide_ref[away, comp, step] for comp in range(6)]
         ref_gap = [other[k] - home[k] for k in range(3)]
         now_gap = [ref_gap[k] + (other[3 + k] - home[3 + k]) for k in range(3)]
         ref_sq = ref_gap[0] * ref_gap[0] + ref_gap[1] * ref_gap[1] + ref_gap[2] * ref_gap[2]
@@ -347,13 +408,20 @@
 
 
 def bond_kernel(
-    words, pairs_ref, count_ref, index_ref, local_ref, ghosts_ref, half_ref, step_ref, bits_ref,
+    words, pairs_in, bits_in, count_ref, ext_ref, half_ref, step_ref,
     displace_ref, velocity_ref, accel_ref,
-    rows_ref, turned_ref, order_ref, wide_ref, total_ref, bit_ref,
+    pairs_ref, bits_ref, rows_ref, turned_ref, sorted_ref, mask_ref, ones_ref, wide_ref,
+    total_ref, bit_ref, load_sems,
 ):
     _, blocks, particles = accel_ref.shape
     pairs = bits_ref.shape[0] // words
-    spread_away(index_ref, local_ref, ghosts_ref, rows_ref, turned_ref, order_ref, wide_ref)
+    loads = [
+        pltpu.make_async_copy(pairs_in, pairs_ref, load_sems.at[0]),
+        pltpu.make_async_copy(bits_in, bits_ref, load_sems.at[1]),
+    ]
+    for load in loads:
+        load.start()
+    spread_away(ext_ref, rows_ref, turned_ref, sorted_ref, mask_ref, ones_ref, wide_ref)
     total_ref[...] = jnp.zeros_like(total_ref)
     sublane = lax.broadcasted_iota(jnp.int32, (SUBLANES, particles), 0)
     for number, (start, _, _) in enumerate(tail_steps(particles)):
@@ -368,6 +436,8 @@
     behind = words - SUBLANES
     keep_front, keep_back = not_own(0, SUBLANES), not_own(SUBLANES, behind)
     count = count_ref[0]
+    for load in loads:
+        load.wait()
 
     def pair_sums(wish):
         slot = jnp.minimum(wish, pairs - 1)
@@ -375,7 +445,7 @@
         home_id = pairs_ref[0, slot]
         away_id = pairs_ref[1, slot]
         home = [
-            jnp.broadcast_to(rows_ref[home_id, pl.ds(comp, 1), :], (SUBLANES, particles))
+            jnp.broadcast_to(ext_ref[home_id, pl.ds(comp, 1), :], (SUBLANES, particles))
             for comp in range(6)
         ]
         apart = jnp.where(home_id == away_id, 0, -1)
@@ -397,33 +467,41 @@
     for comp in range(3):
         for block in range(blocks):
             accel_ref[comp, pl.ds(block, 1), :] = accel[block, comp : comp + 1]
-            displace_ref[comp, pl.ds(block, 1), :] = local_ref[block, pl.ds(3 + comp, 1), :]
+            displace_ref[comp, pl.ds(block, 1), :] = ext_ref[block, pl.ds(3 + comp, 1), :]
         velocity_ref[comp] = half_ref[comp] + 0.5 * step_ref[...] * accel_ref[comp]
 
 
-def bond_step(index, local, ghosts, half, step, pair_blocks, pair_count, bond_bits):
+def bond_step(ext, half, step, pair_blocks, pair_count, bond_bits):
     blocks, particles = step.shape
-    extended = index.shape[0] + blocks
+    extended = ext.shape[0]
     words, pairs = bond_bits.shape[0:2]
     shape = jax.ShapeDtypeStruct((3, blocks, particles), jnp.float32)
     smem = pl.BlockSpec(memory_space=pltpu.SMEM)
     vmem = pl.BlockSpec(memory_space=pltpu.VMEM)
+    hbm = pl.BlockSpec(memory_space=pltpu.HBM)
     groups = particles // SUBLANES
+    batch = particles // (4 * SUBLANES)
+    halves = -(-extended // (2 * batch))
     return pl.pallas_call(
         functools.partial(bond_kernel, words),
         out_shape=(shape, shape, shape),
-        in_specs=[smem, smem, smem, vmem, vmem, vmem, vmem, vmem],
+        in_specs=[hbm, hbm, smem, vmem, vmem, vmem],
         out_specs=(vmem, vmem, vmem),
         scratch_shapes=[
-            pltpu.VMEM((extended, SUBLANES, particles), jnp.float32),
-            pltpu.VMEM((particles, particles), jnp.float32),
-            pltpu.VMEM((extended * SUBLANES // particles * groups, SUBLANES, particles), jnp.float32),
-            pltpu.VMEM((extended, groups, 6, SUBLANES, particles), jnp.float32),
+            pltpu.SMEM(pair_blocks.shape, jnp.int32),
+            pltpu.VMEM((words * pairs, particles), jnp.int32),
+            pltpu.VMEM((2 * halves * particles, particles), jnp.float32),
+            pltpu.VMEM((2 * halves, particles, particles), jnp.float32),
+            pltpu.VMEM((halves, groups // 2, 2 * SUBLANES, 2 * particles), jnp.bfloat16),
+            pltpu.VMEM((batch, 6, 2 * SUBLANES, 2 * particles), jnp.bfloat16),
+            pltpu.VMEM((2 * particles, 2 * particles), jnp.bfloat16),
+            pltpu.VMEM((2 * halves * batch, 6, groups, SUBLANES, particles), jnp.float32),
             pltpu.VMEM((blocks, 3, SUBLANES, particles), jnp.float32),
             pltpu.VMEM((len(tail_steps(particles)), SUBLANES, particles), jnp.int32),
+            pltpu.SemaphoreType.DMA((2,)),
         ],
         compiler_params=pltpu.CompilerParams(vmem_limit_bytes=40 * 1024 * 1024),
-    )(pair_blocks, pair_count, index, local, ghosts, half, step, bond_bits.reshape(words * pairs, particles))
+    )(pair_blocks, bond_bits.reshape(words * pairs, particles), pair_count, ext, half, step)
 
 
 def per_device(
@@ -437,29 +515,10 @@
     pair_count,
     bond_bits,
 ):
-    blocks = ref_pos.shape[0]
     sizes = tuple(lax.axis_size(name) for name in AXES)
-    places = [lax.axis_index(name) for name in AXES]
     turned = [array.transpose(1, 0, 2) for array in (ref_pos, displace, velocity, acceleration)]
-    local, ghosts, half, step = exchange(sizes, new_owner, ghost_ids, *turned)
-    ghost_dev = ghost_ids // blocks
-    ghost_places = (
-        ghost_dev // (sizes[1] * sizes[2]),
-        ghost_dev // sizes[2] % sizes[1],
-        ghost_dev % sizes[2],
-    )
-    moves = []
-    for ghost, place, size in zip(ghost_places, places, sizes):
-        apart = (ghost - place) % size
-        moves.append(jnp.where(apart == size - 1, -1, apart) if size > 2 else apart)
-    ghost_cell = cell_of(places, moves, sizes)
-    order = jnp.arange(ghost_ids.shape[0])
-    repeats = (ghost_dev[:, None] == ghost_dev[None, :]) & (order[None, :] < order[:, None])
-    index = ghost_cell * REQUESTS + jnp.sum(repeats.astype(jnp.int32), axis=1)
-    ghosts = ghosts.reshape((-1,) + ghosts.shape[2:])
-    results = bond_step(
-        index, local, ghosts, half, step, pair_blocks, pair_count, bond_bits.transpose(1, 0, 2)
-    )
+    ext, half, step = exchange(sizes, new_owner, ghost_ids, *turned)
+    results = bond_step(ext, half, step, pair_blocks, pair_count, bond_bits.transpose(1, 0, 2))
     return tuple(array.transpose(1, 0, 2) for array in results)
 
 

time: 50.7 us -> 44.4 us (0.88)
  the two profiles are of different devices: /device:TPU:16 before, /device:TPU:9 now
where the time goes in v1:
time: 44.4 us; the launch traced here: 43.9 us
  Pallas kernels  36.4 us (82%)
  local copies, waits for them, and re-layouts  6.13 us (14%)
  between operations  1.31 us (3%)
    pallas_call x1, Pallas kernels, bond_step(): pl.pallas_call(functools.partial(bond_kernel, words), out_shape=(shape, s...  19.8 us
    pallas_call x1, Pallas kernels, exchange(): pl.pallas_call(functools.partial(exchange_kernel, sizes), out_shape=(jax....  16.7 us
    unnamed x16, local copies, waits for them, and re-layouts  6.13 us

profile of v1, /device:TPU:9, one launch (start us, length us, event | category | flops | bytes accessed | tf_op | source)
XLA Modules:
  0.0 43.9 jit_solution(9783482069634728887)
XLA Ops:
  1.3 0.0 copy-start.1
  1.3 0.7 %copy-done.1 = f32[8,3,128]{2,0,1:T(8,128)S(1)} copy-done((f32[8,3,128]{2,0,1:T(8,128)S(1)}, f32[8,3,128]{2,0,1:T(8,128)}, u32[]{:S(2)}) %copy-start.1) | copy-done | bytes 12312
  2.0 0.0 copy-start.2
  2.0 0.7 %copy-done.2 = f32[8,3,128]{2,0,1:T(8,128)S(1)} copy-done((f32[8,3,128]{2,0,1:T(8,128)S(1)}, f32[8,3,128]{2,0,1:T(8,128)}, u32[]{:S(2)}) %copy-start.2) | copy-done | bytes 12312
  2.7 0.0 copy-start.3
  2.7 0.7 %copy-done.3 = f32[8,3,128]{2,0,1:T(8,128)S(1)} copy-done((f32[8,3,128]{2,0,1:T(8,128)S(1)}, f32[8,3,128]{2,0,1:T(8,128)}, u32[]{:S(2)}) %copy-start.3) | copy-done | bytes 12312
  3.4 0.0 copy-start.4
  3.4 0.7 %copy-done.4 = f32[8,3,128]{2,0,1:T(8,128)S(1)} copy-done((f32[8,3,128]{2,0,1:T(8,128)S(1)}, f32[8,3,128]{2,0,1:T(8,128)}, u32[]{:S(2)}) %copy-start.4) | copy-done | bytes 12312
  4.1 0.0 copy-start.6
  4.1 0.7 %copy-done.6 = s32[8]{0:T(128)S(1)} copy-done((s32[8]{0:T(128)S(1)}, s32[8]{0:T(128)}, u32[]{:S(2)}) %copy-start.6) | copy-done | bytes 56
  4.8 0.0 copy-start.7
  4.8 0.7 %copy-done.7 = s32[24]{0:T(128)S(1)} copy-done((s32[24]{0:T(128)S(1)}, s32[24]{0:T(128)}, u32[]{:S(2)}) %copy-start.7) | copy-done | bytes 120
  5.4 16.7 %shard_map.112 = (f32[32,8,128]{2,1,0:T(8,128)S(1)}, f32[3,8,128]{2,1,0:T(8,128)S(1)}, f32[8,128]{1,0:T(8,128)S(1)}) custom-call(s32[8]{0:T(128)S(1)} %copy-done.6, s32[24]{0:T(128)S(1)} %copy-done.7, f32[3,8,128]{2,1,0:T(8,128)S(1)} %bitcast.11, f32[3,8,128]{2,1,0:T(8,128)S(1)} %bitcast.12, f32[3,8,128]{2,1,0:T(8,128)S(1)} %bitcast.13, ...), custom_call_target="tpu_custom_call" | custom-call | tf_op jit(solution)/shard_map/pallas_call | solution.py:290
  22.1 0.0 copy-start
  22.1 1.3 %copy-done = s32[216,12,128]{2,0,1:T(8,128)S(1)} copy-done((s32[216,12,128]{2,0,1:T(8,128)S(1)}, s32[216,12,128]{2,0,1:T(8,128)}, u32[]{:S(2)}) %copy-start) | copy-done | bytes 1327128
  23.4 0.0 copy-start.5
  23.4 0.7 %copy-done.5 = s32[2,216]{1,0:T(2,128)S(1)} copy-done((s32[2,216]{1,0:T(2,128)S(1)}, s32[2,216]{1,0:T(2,128)}, u32[]{:S(2)}) %copy-start.5) | copy-done | bytes 1752
  24.1 19.8 %shard_map.113 = (f32[3,8,128]{2,1,0:T(8,128)}, f32[3,8,128]{2,1,0:T(8,128)}, f32[3,8,128]{2,1,0:T(8,128)}) custom-call(s32[2,216]{1,0:T(2,128)S(1)} %copy-done.5, s32[2592,128]{1,0:T(8,128)S(1)} %bitcast.10, s32[1]{0:T(128)S(6)} %copy.12.count_ref, f32[32,8,128]{2,1,0:T(8,128)S(1)} %get-tuple-element.9.ext_ref, ...), custom_call_target="tpu_custom_call" | custom-call | tf_op jit(solution)/shard_map/pallas_call | solution.py:485
Async XLA Ops:
  1.3 0.7 %copy-start.1 = (f32[8,3,128]{2,0,1:T(8,128)S(1)}, f32[8,3,128]{2,0,1:T(8,128)}, u32[]{:S(2)}) copy-start(f32[8,3,128]{2,0,1:T(8,128)} %param.9) | copy-start | bytes 36868
  2.0 0.7 %copy-start.2 = (f32[8,3,128]{2,0,1:T(8,128)S(1)}, f32[8,3,128]{2,0,1:T(8,128)}, u32[]{:S(2)}) copy-start(f32[8,3,128]{2,0,1:T(8,128)} %param.10) | copy-start | bytes 36868
  2.7 0.7 %copy-start.3 = (f32[8,3,128]{2,0,1:T(8,128)S(1)}, f32[8,3,128]{2,0,1:T(8,128)}, u32[]{:S(2)}) copy-start(f32[8,3,128]{2,0,1:T(8,128)} %param.11) | copy-start | bytes 36868
  3.4 0.7 %copy-start.4 = (f32[8,3,128]{2,0,1:T(8,128)S(1)}, f32[8,3,128]{2,0,1:T(8,128)}, u32[]{:S(2)}) copy-start(f32[8,3,128]{2,0,1:T(8,128)} %param.12) | copy-start | bytes 36868
  4.1 0.7 %copy-start.6 = (s32[8]{0:T(128)S(1)}, s32[8]{0:T(128)}, u32[]{:S(2)}) copy-start(s32[8]{0:T(128)} %owner_in.1) | copy-start | bytes 100
  4.8 0.7 %copy-start.7 = (s32[24]{0:T(128)S(1)}, s32[24]{0:T(128)}, u32[]{:S(2)}) copy-start(s32[24]{0:T(128)} %ghost_in.1) | copy-start | bytes 292
  22.1 1.3 %copy-start = (s32[216,12,128]{2,0,1:T(8,128)S(1)}, s32[216,12,128]{2,0,1:T(8,128)}, u32[]{:S(2)}) copy-start(s32[216,12,128]{2,0,1:T(8,128)} %param.17) | copy-start | bytes 3981316
  23.4 0.7 %copy-start.5 = (s32[2,216]{1,0:T(2,128)S(1)}, s32[2,216]{1,0:T(2,128)}, u32[]{:S(2)}) copy-start(s32[2,216]{1,0:T(2,128)} %pairs_in.1) | copy-start | bytes 5188

commit v2 on v1

--- a/solution.py
+++ b/solution.py
@@ -51,25 +51,14 @@
     return [steps for steps in every if steps != (0, 0, 0)]
 
 
-def cell_target(places, ranks, sizes):
-    target = []
-    for place, rank, size in zip(places, ranks, sizes):
-        if size < 3:
-            target.append(jnp.int32(rank))
-        else:
-            first = (size - place) // size
-            last = (place + 1) // size
-            target.append((place + (rank + 6 - 2 * first - last) % 3 - 1 + size) % size)
-    return target
-
-
 def exchange_kernel(
     sizes,
     owner_in, ghost_in, ref_in, disp_in, vel_in, acc_in,
+    ext_out, half_out, step_out,
+    owner_ref, ghost_ref, ref_ref, disp_ref, vel_ref, acc_ref,
+    arrived_ref, card_ref, peak_ref, pack_ref, ghosts_ref, list_ref, ask_ref, flat_ref,
     ext_ref, half_ref, step_ref,
-    owner_ref, ghost_ref, ref_ref, disp_ref, vel_ref, acc_ref,
-    arrived_ref, card_ref, pack_ref, ghosts_ref, list_ref, ask_ref, flat_ref,
-    send_sems, recv_sems, load_sems,
+    send_sems, recv_sems, load_sems, store_sems,
 ):
     dims, blocks, particles = ref_ref.shape
     inner = (owner_ref, ghost_ref, ref_ref, disp_ref, vel_ref, acc_ref)
@@ -81,18 +70,22 @@
     for load in loads:
         load.start()
     total = sizes[0] * sizes[1] * sizes[2]
-    steps_all = neighbour_steps(sizes)
+    steps_all = sorted(neighbour_steps(sizes), key=lambda steps: -abs(steps[0]))
     cells = len(steps_all) + 1
-    extents = [len(reach(size)) for size in sizes]
-    ranks_all = [
-        (x, y, z) for x in range(extents[0]) for y in range(extents[1]) for z in range(extents[2])
-    ]
+    far = total - cells if total <= UNROLLED else total - 1
     places = [lax.axis_index(name) for name in AXES]
     myself = (places[0] * sizes[1] + places[1]) * sizes[2] + places[2]
     mine = cell_of(places, (0, 0, 0), sizes)
+    routes = {}
+    for steps in steps_all:
+        target = [(place + step) % size for place, step, size in zip(places, steps, sizes)]
+        back = [-step for step in steps]
+        routes[steps] = (
+            tuple(target), cell_of(places, steps, sizes), cell_of(target, back, sizes)
+        )
     sources = (ref_ref, disp_ref, vel_ref, acc_ref)
 
-    def to_others(action):
+    def to_others(action, near):
         if total <= UNROLLED:
             coords = [
                 [(place + step) % size for step in range(size)]
@@ -101,7 +94,9 @@
             for x in range(sizes[0]):
                 for y in range(sizes[1]):
                     for z in range(sizes[2]):
-                        if (x, y, z) != (0, 0, 0):
+                        wraps = zip((x, y, z), sizes)
+                        beside = all(step in (0, 1, size - 1) for step, size in wraps)
+                        if (x, y, z) != (0, 0, 0) and (near or not beside):
                             action((coords[0][x], coords[1][y], coords[2][z]))
         else:
 
@@ -113,9 +108,11 @@
 
             lax.fori_loop(1, total, act, 0)
 
+    peak_ref[...] = jnp.zeros_like(peak_ref)
     barrier = pltpu.get_barrier_semaphore()
     to_others(
-        lambda target: pl.semaphore_signal(barrier, inc=1, device_id=target, device_id_type=MESH)
+        lambda target: pl.semaphore_signal(barrier, inc=1, device_id=target, device_id_type=MESH),
+        True,
     )
 
     for load in loads:
@@ -128,16 +125,18 @@
             leavers[order] += block * leaves * jnp.where(seen == order, 1, 0)
         seen += leaves
     speeds = jnp.max(jnp.abs(vel_ref[...]), axis=0)
-    card_ref[myself, pl.ds(0, 1), :] = jnp.max(speeds, axis=0, keepdims=True)
+    peak = jnp.max(speeds, axis=0, keepdims=True)
+    card_ref[mine, pl.ds(0, 1), :] = peak
+    peak_ref[myself] = peak
     for order in range(MOVERS):
         owner = jnp.full((1, particles), owner_ref[leavers[order]], jnp.int32)
-        card_ref[myself, pl.ds(OWNER_ROW + order, 1), :] = owner.astype(jnp.float32)
+        card_ref[mine, pl.ds(OWNER_ROW + order, 1), :] = owner.astype(jnp.float32)
     ghosts = ghost_ref.shape[0]
     lane = lax.broadcasted_iota(jnp.int32, (1, particles), 1)
     wish = jnp.full((1, particles), -blocks, jnp.int32)
     for ghost in range(ghosts):
         wish = jnp.where(lane == ghost, ghost_ref[ghost], wish)
-    card_ref[myself, pl.ds(GHOST_ROW, 1), :] = wish.astype(jnp.float32)
+    card_ref[mine, pl.ds(GHOST_ROW, 1), :] = wish.astype(jnp.float32)
     for order in range(MOVERS):
         for part, source in enumerate(sources):
             for dim in range(dims):
@@ -146,40 +145,54 @@
 
     pl.semaphore_wait(barrier, total - 1)
 
-    def send_card(target):
+    def send_peak(target):
         pltpu.make_async_remote_copy(
-            src_ref=card_ref.at[myself],
-            dst_ref=card_ref.at[myself],
-            send_sem=send_sems.at[0],
-            recv_sem=recv_sems.at[0],
+            src_ref=peak_ref.at[myself],
+            dst_ref=peak_ref.at[myself],
+            send_sem=send_sems.at[3],
+            recv_sem=recv_sems.at[3],
             device_id=target,
             device_id_type=MESH,
         ).start()
 
     def send_halo(steps, source_of, ref, kind):
-        target = [(place + step) % size for place, step, size in zip(places, steps, sizes)]
-        back = [-step for step in steps]
+        target, cell, landing = routes[steps]
         pltpu.make_async_remote_copy(
-            src_ref=source_of(cell_of(places, steps, sizes)),
-            dst_ref=ref.at[cell_of(target, back, sizes)],
+            src_ref=source_of(cell),
+            dst_ref=ref.at[landing],
             send_sem=send_sems.at[kind],
             recv_sem=recv_sems.at[kind],
-            device_id=tuple(target),
+            device_id=target,
             device_id_type=MESH,
         ).start()
 
-    def all_bytes(ref, sem):
-        part = ref.at[pl.ds(0, ref.shape[0] - 1)]
+    def all_bytes(ref, sem, number):
+        part = ref.at[pl.ds(0, number)]
         return pltpu.make_async_copy(part, part, sem)
 
-    to_others(send_card)
+    for steps in steps_all:
+        send_halo(steps, lambda cell: card_ref.at[mine], card_ref, 0)
+    if far:
+        to_others(send_peak, False)
     for steps in steps_all:
         send_halo(steps, lambda cell: arrived_ref.at[mine], arrived_ref, 1)
 
-    all_bytes(card_ref, recv_sems.at[0]).wait()
-    fastest = jnp.max(jnp.max(card_ref[:, pl.ds(0, 1), :], axis=0), axis=1, keepdims=True)
+    all_bytes(card_ref, recv_sems.at[0], cells - 1).wait()
+    if far:
+        all_bytes(peak_ref, recv_sems.at[3], far).wait()
+    highest = jnp.maximum(
+        jnp.max(peak_ref[...], axis=0), jnp.max(card_ref[:, pl.ds(0, 1), :], axis=0)
+    )
+    fastest = jnp.max(highest, axis=1, keepdims=True)
     timestep = jnp.broadcast_to(courant / (fastest + 1e-06), (blocks, particles))
     step_ref[...] = timestep
+    stores = [
+        pltpu.make_async_copy(source, target, store_sems.at[number])
+        for number, (source, target) in enumerate(
+            ((step_ref, step_out), (half_ref, half_out), (ext_ref, ext_out))
+        )
+    ]
+    stores[0].start()
 
     name = myself.astype(jnp.float32)
     slot = lax.broadcasted_iota(jnp.int32, (blocks, particles), 0).astype(jnp.float32)
@@ -187,15 +200,13 @@
     own_start = jnp.zeros((1, particles), jnp.float32)
     goals = []
     list_ref[...] = jnp.zeros_like(list_ref)
-    for cell, ranks in enumerate(ranks_all):
-        target = cell_target(places, ranks, sizes)
-        device = (target[0] * sizes[1] + target[1]) * sizes[2] + target[2]
-        list_ref[pl.ds(cell, 1), :] = card_ref[device, pl.ds(GHOST_ROW, 1), :]
+    for cell in range(cells):
+        list_ref[pl.ds(cell, 1), :] = card_ref[cell, pl.ds(GHOST_ROW, 1), :]
         own = jnp.where(mine == cell, 1.0, 0.0)
         own_start = own_start + own * count
         count = count + own * (blocks - MOVERS)
         for order in range(MOVERS):
-            hit = card_ref[device, pl.ds(OWNER_ROW + order, 1), :] == name
+            hit = card_ref[cell, pl.ds(OWNER_ROW + order, 1), :] == name
             goals.append(jnp.where(hit, count, -1.0))
             count = count + jnp.where(hit, 1.0, 0.0)
 
@@ -213,7 +224,7 @@
         slots = jnp.sum(jnp.where(fits, ids - owners * blocks, 0.0), axis=1, keepdims=True)
         ask_ref[request] = jnp.broadcast_to(slots, ids.shape)
 
-    all_bytes(arrived_ref, recv_sems.at[1]).wait()
+    all_bytes(arrived_ref, recv_sems.at[1], cells - 1).wait()
     settled = [jnp.zeros((blocks, particles), jnp.float32) for _ in range(STATE)]
     for cell in range(cells):
         for order in range(MOVERS):
@@ -255,6 +266,7 @@
 
     for steps in steps_all:
         send_halo(steps, lambda cell: pack_ref.at[cell], ghosts_ref, 2)
+    stores[1].start()
     taken = []
     for ghost in range(ghosts):
         device = lax.div(ghost_ref[ghost], blocks)
@@ -270,13 +282,18 @@
         taken.append((cell_of(places, moves, sizes) * REQUESTS + repeats, device))
     for ghost in range(ghosts):
         ext_ref[blocks + ghost] = jnp.zeros((SUBLANES, particles), jnp.float32)
-    all_bytes(ghosts_ref, recv_sems.at[2]).wait()
+    all_bytes(ghosts_ref, recv_sems.at[2], cells - 1).wait()
     for ghost, (index, _) in enumerate(taken):
         rows = ghosts_ref[lax.div(index, REQUESTS), lax.rem(index, REQUESTS)]
         ext_ref[blocks + ghost, pl.ds(0, comps), :] = rows
-    all_bytes(card_ref, send_sems.at[0]).wait()
-    all_bytes(arrived_ref, send_sems.at[1]).wait()
-    all_bytes(ghosts_ref, send_sems.at[2]).wait()
+    stores[2].start()
+    all_bytes(card_ref, send_sems.at[0], cells - 1).wait()
+    all_bytes(arrived_ref, send_sems.at[1], cells - 1).wait()
+    all_bytes(ghosts_ref, send_sems.at[2], cells - 1).wait()
+    if far:
+        all_bytes(peak_ref, send_sems.at[3], far).wait()
+    for store in stores:
+        store.wait()
 
 
 def exchange(sizes, new_owner, ghost_ids, ref_pos, displace, velocity, acceleration):
@@ -286,16 +303,16 @@
     padded = -(-cells // SUBLANES) * SUBLANES
     ghosts = ghost_ids.shape[0]
     hbm = pl.BlockSpec(memory_space=pltpu.HBM)
-    vmem = pl.BlockSpec(memory_space=pltpu.VMEM)
+    outs = (
+        jax.ShapeDtypeStruct((blocks + ghosts, SUBLANES, particles), jnp.float32),
+        jax.ShapeDtypeStruct((dims, blocks, particles), jnp.float32),
+        jax.ShapeDtypeStruct((blocks, particles), jnp.float32),
+    )
     return pl.pallas_call(
         functools.partial(exchange_kernel, sizes),
-        out_shape=(
-            jax.ShapeDtypeStruct((blocks + ghosts, SUBLANES, particles), jnp.float32),
-            jax.ShapeDtypeStruct((dims, blocks, particles), jnp.float32),
-            jax.ShapeDtypeStruct((blocks, particles), jnp.float32),
-        ),
+        out_shape=outs,
         in_specs=[hbm] * 6,
-        out_specs=(vmem, vmem, vmem),
+        out_specs=(hbm, hbm, hbm),
         scratch_shapes=[
             pltpu.SMEM(new_owner.shape, jnp.int32),
             pltpu.SMEM(ghost_ids.shape, jnp.int32),
@@ -304,18 +321,21 @@
             pltpu.VMEM(ref_pos.shape, jnp.float32),
             pltpu.VMEM(ref_pos.shape, jnp.float32),
             pltpu.VMEM((cells, MOVERS * STATE, particles), jnp.float32),
-            pltpu.VMEM((total, CARD, particles), jnp.float32),
+            pltpu.VMEM((cells, CARD, particles), jnp.float32),
+            pltpu.VMEM((total, 1, particles), jnp.float32),
             pltpu.VMEM((cells, REQUESTS, 2 * dims, particles), jnp.float32),
             pltpu.VMEM((cells, REQUESTS, 2 * dims, particles), jnp.float32),
             pltpu.VMEM((padded, particles), jnp.float32),
             pltpu.VMEM((REQUESTS, padded, particles), jnp.float32),
             pltpu.VMEM((2 * dims * blocks, particles), jnp.float32),
+            *[pltpu.VMEM(out.shape, jnp.float32) for out in outs],
+            pltpu.SemaphoreType.DMA((4,)),
+            pltpu.SemaphoreType.DMA((4,)),
+            pltpu.SemaphoreType.DMA((6,)),
             pltpu.SemaphoreType.DMA((3,)),
-            pltpu.SemaphoreType.DMA((3,)),
-            pltpu.SemaphoreType.DMA((6,)),
         ],
         compiler_params=pltpu.CompilerParams(
-            collective_id=0, has_side_effects=True, vmem_limit_bytes=16 * 1024 * 1024
+            collective_id=0, has_side_effects=True, vmem_limit_bytes=64 * 1024 * 1024
         ),
     )(new_owner, ghost_ids, ref_pos, displace, velocity, acceleration)
 
@@ -408,19 +428,22 @@
 
 
 def bond_kernel(
-    words, pairs_in, bits_in, count_ref, ext_ref, half_ref, step_ref,
+    words, pairs_in, bits_in, ext_in, half_in, step_in, count_ref,
     displace_ref, velocity_ref, accel_ref,
-    pairs_ref, bits_ref, rows_ref, turned_ref, sorted_ref, mask_ref, ones_ref, wide_ref,
+    pairs_ref, bits_ref, ext_ref, half_ref, step_ref, rows_ref, turned_ref, sorted_ref, mask_ref, ones_ref, wide_ref,
     total_ref, bit_ref, load_sems,
 ):
     _, blocks, particles = accel_ref.shape
     pairs = bits_ref.shape[0] // words
+    outer = (ext_in, pairs_in, bits_in, half_in, step_in)
+    inner = (ext_ref, pairs_ref, bits_ref, half_ref, step_ref)
     loads = [
-        pltpu.make_async_copy(pairs_in, pairs_ref, load_sems.at[0]),
-        pltpu.make_async_copy(bits_in, bits_ref, load_sems.at[1]),
+        pltpu.make_async_copy(source, target, load_sems.at[number])
+        for number, (source, target) in enumerate(zip(outer, inner))
     ]
     for load in loads:
         load.start()
+    loads[0].wait()
     spread_away(ext_ref, rows_ref, turned_ref, sorted_ref, mask_ref, ones_ref, wide_ref)
     total_ref[...] = jnp.zeros_like(total_ref)
     sublane = lax.broadcasted_iota(jnp.int32, (SUBLANES, particles), 0)
@@ -436,7 +459,7 @@
     behind = words - SUBLANES
     keep_front, keep_back = not_own(0, SUBLANES), not_own(SUBLANES, behind)
     count = count_ref[0]
-    for load in loads:
+    for load in loads[1:]:
         load.wait()
 
     def pair_sums(wish):
@@ -485,11 +508,14 @@
     return pl.pallas_call(
         functools.partial(bond_kernel, words),
         out_shape=(shape, shape, shape),
-        in_specs=[hbm, hbm, smem, vmem, vmem, vmem],
+        in_specs=[hbm, hbm, hbm, hbm, hbm, smem],
         out_specs=(vmem, vmem, vmem),
         scratch_shapes=[
             pltpu.SMEM(pair_blocks.shape, jnp.int32),
             pltpu.VMEM((words * pairs, particles), jnp.int32),
+            pltpu.VMEM(ext.shape, jnp.float32),
+            pltpu.VMEM(half.shape, jnp.float32),
+            pltpu.VMEM(step.shape, jnp.float32),
             pltpu.VMEM((2 * halves * particles, particles), jnp.float32),
             pltpu.VMEM((2 * halves, particles, particles), jnp.float32),
             pltpu.VMEM((halves, groups // 2, 2 * SUBLANES, 2 * particles), jnp.bfloat16),
@@ -498,10 +524,10 @@
             pltpu.VMEM((2 * halves * batch, 6, groups, SUBLANES, particles), jnp.float32),
             pltpu.VMEM((blocks, 3, SUBLANES, particles), jnp.float32),
             pltpu.VMEM((len(tail_steps(particles)), SUBLANES, particles), jnp.int32),
-            pltpu.SemaphoreType.DMA((2,)),
+            pltpu.SemaphoreType.DMA((5,)),
         ],
-        compiler_params=pltpu.CompilerParams(vmem_limit_bytes=40 * 1024 * 1024),
-    )(pair_blocks, bond_bits.reshape(words * pairs, particles), pair_count, ext, half, step)
+        compiler_params=pltpu.CompilerParams(vmem_limit_bytes=64 * 1024 * 1024),
+    )(pair_blocks, bond_bits.reshape(words * pairs, particles), ext, half, step, pair_count)
 
 
 def per_device(

time: 44.4 us -> 39.2 us (0.88)
  local copies, waits for them, and re-layouts: 6.13 us -> 0 us
  Pallas kernels: 36.4 us -> 37.7 us
    unnamed x16 -> x0, local copies, waits for them, and re-layouts: 6.13 us -> none
    pallas_call x1, Pallas kernels: 19.8 us -> 20.6 us  [bond_step(): pl.pallas_call(functools.partial(bond_kernel, words), out_shape=(shape, s...]
where the time goes in v2:
time: 39.2 us; the launch traced here: 39 us
  Pallas kernels  37.7 us (96%)
  between operations  1.29 us (3%)
    pallas_call x1, Pallas kernels, bond_step(): pl.pallas_call(functools.partial(bond_kernel, words), out_shape=(shape, s...  20.6 us
    pallas_call x1, Pallas kernels, exchange(): pl.pallas_call(functools.partial(exchange_kernel, sizes), out_shape=outs,...  17.1 us

profile of v2, /device:TPU:9, one launch (start us, length us, event | category | flops | bytes accessed | tf_op | source)
XLA Modules:
  0.0 39.0 jit_solution(4583679519574984024)
XLA Ops:
  1.3 17.1 %shard_map.112 = (f32[32,8,128]{2,1,0:T(8,128)}, f32[3,8,128]{2,1,0:T(8,128)}, f32[8,128]{1,0:T(8,128)}) custom-call(s32[8]{0:T(128)} %owner_in.1, s32[24]{0:T(128)} %ghost_in.1, f32[3,8,128]{2,1,0:T(8,128)} %bitcast.11, f32[3,8,128]{2,1,0:T(8,128)} %bitcast.12, f32[3,8,128]{2,1,0:T(8,128)} %bitcast.13, f32[3,8,128]{2,1,0:T(8,128)} %bitcast.14), custom_call_target="tpu_custom_call" | custom-call | tf_op jit(solution)/shard_map/pallas_call | solution.py:311
  18.4 20.6 %shard_map.113 = (f32[3,8,128]{2,1,0:T(8,128)}, f32[3,8,128]{2,1,0:T(8,128)}, f32[3,8,128]{2,1,0:T(8,128)}) custom-call(s32[2,216]{1,0:T(2,128)} %pairs_in.1, s32[2592,128]{1,0:T(8,128)} %bitcast.10, f32[32,8,128]{2,1,0:T(8,128)} %get-tuple-element.9.ext_in, f32[3,8,128]{2,1,0:T(8,128)} %get-tuple-element.10.half_in, f32[8,128]{1,0:T(8,128)} %get-tuple-element.11.step_in, ...), custom_call_target="tpu_custom_call" | custom-call | tf_op jit(solution)/shard_map/pallas_call | solution.py:508

commit v3 on v2

--- a/solution.py
+++ b/solution.py
@@ -24,7 +24,7 @@
 GHOST_ROW = OWNER_ROW + MOVERS
 CARD = GHOST_ROW + 1
 UNROLLED = 64
-TOGETHER = 2
+TOGETHER = 4
 
 
 def reach(size):
@@ -340,7 +340,7 @@
     )(new_owner, ghost_ids, ref_pos, displace, velocity, acceleration)
 
 
-def spread_away(ext_ref, rows_ref, turned_ref, sorted_ref, mask_ref, ones_ref, wide_ref):
+def spread_away(ready, ext_ref, rows_ref, turned_ref, sorted_ref, mask_ref, ones_ref, wide_ref):
     extended, comps, particles = ext_ref.shape
     used = wide_ref.shape[1]
     groups = wide_ref.shape[2]
@@ -349,6 +349,15 @@
     batch = particles // stride
     aligned = SUBLANES * WORD_BITS
     rows_ref[...] = jnp.zeros_like(rows_ref)
+    lane = lax.broadcasted_iota(jnp.int32, mask_ref.shape[2:], 1) % particles
+    for block in range(batch):
+        for comp in range(used):
+            keep = jnp.logical_and(lane // stride == block, lane % comps == comp)
+            mask_ref[block, comp] = jnp.where(keep, 1.0, 0.0).astype(jnp.bfloat16)
+    above = lax.broadcasted_iota(jnp.int32, ones_ref.shape, 0) // particles
+    beside = lax.broadcasted_iota(jnp.int32, ones_ref.shape, 1) // particles
+    ones_ref[...] = jnp.where(above == beside, 1.0, 0.0).astype(jnp.bfloat16)
+    ready()
     for block in range(extended):
         rest = ext_ref[block]
         for term in range(3):
@@ -369,15 +378,6 @@
                     parts.append(turned_ref[number, pl.ds(start, SUBLANES), :])
             both = jnp.concatenate(parts, axis=0).astype(jnp.bfloat16)
             sorted_ref[half, pair, :, pl.ds(column, particles)] = both
-    lane = lax.broadcasted_iota(jnp.int32, mask_ref.shape[2:], 1) % particles
-    for block in range(batch):
-        for comp in range(used):
-            keep = jnp.logical_and(lane // stride == block, lane % comps == comp)
-            mask_ref[block, comp] = jnp.where(keep, 1.0, 0.0).astype(jnp.bfloat16)
-    above = lax.broadcasted_iota(jnp.int32, ones_ref.shape, 0) // particles
-    beside = lax.broadcasted_iota(jnp.int32, ones_ref.shape, 1) // particles
-    ones_ref[...] = jnp.where(above == beside, 1.0, 0.0).astype(jnp.bfloat16)
-
     def spread_half(half, carry):
         table = sorted_ref[half]
         for block in range(batch):
@@ -443,12 +443,14 @@
     ]
     for load in loads:
         load.start()
-    loads[0].wait()
-    spread_away(ext_ref, rows_ref, turned_ref, sorted_ref, mask_ref, ones_ref, wide_ref)
     total_ref[...] = jnp.zeros_like(total_ref)
     sublane = lax.broadcasted_iota(jnp.int32, (SUBLANES, particles), 0)
     for number, (start, _, _) in enumerate(tail_steps(particles)):
         bit_ref[number] = jnp.left_shift(1, (sublane + start) % WORD_BITS)
+
+    spread_away(
+        loads[0].wait, ext_ref, rows_ref, turned_ref, sorted_ref, mask_ref, ones_ref, wide_ref
+    )
 
     def not_own(first, rows):
         word = lax.broadcasted_iota(jnp.int32, (rows, particles), 0) + first

time: 39.2 us -> 37.3 us (0.952)
  the two profiles are of different devices: /device:TPU:9 before, /device:TPU:25 now
where the time goes in v3:
time: 37.3 us; the launch traced here: 37.1 us
  Pallas kernels  35.8 us (96%)
  between operations  1.29 us (3%)
    pallas_call x1, Pallas kernels, bond_step(): pl.pallas_call(functools.partial(bond_kernel, words), out_shape=(shape, s...  19.7 us
    pallas_call x1, Pallas kernels, exchange(): pl.pallas_call(functools.partial(exchange_kernel, sizes), out_shape=outs,...  16.1 us

profile of v3, /device:TPU:25, one launch (start us, length us, event | category | flops | bytes accessed | tf_op | source)
XLA Modules:
  0.0 37.1 jit_solution(16321448940029207793)
XLA Ops:
  1.3 16.1 %shard_map.112 = (f32[32,8,128]{2,1,0:T(8,128)}, f32[3,8,128]{2,1,0:T(8,128)}, f32[8,128]{1,0:T(8,128)}) custom-call(s32[8]{0:T(128)} %owner_in.1, s32[24]{0:T(128)} %ghost_in.1, f32[3,8,128]{2,1,0:T(8,128)} %bitcast.11, f32[3,8,128]{2,1,0:T(8,128)} %bitcast.12, f32[3,8,128]{2,1,0:T(8,128)} %bitcast.13, f32[3,8,128]{2,1,0:T(8,128)} %bitcast.14), custom_call_target="tpu_custom_call" | custom-call | tf_op jit(solution)/shard_map/pallas_call | solution.py:311
  17.4 19.7 %shard_map.113 = (f32[3,8,128]{2,1,0:T(8,128)}, f32[3,8,128]{2,1,0:T(8,128)}, f32[3,8,128]{2,1,0:T(8,128)}) custom-call(s32[2,216]{1,0:T(2,128)} %pairs_in.1, s32[2592,128]{1,0:T(8,128)} %bitcast.10, f32[32,8,128]{2,1,0:T(8,128)} %get-tuple-element.9.ext_in, f32[3,8,128]{2,1,0:T(8,128)} %get-tuple-element.10.half_in, f32[8,128]{1,0:T(8,128)} %get-tuple-element.11.step_in, ...), custom_call_target="tpu_custom_call" | custom-call | tf_op jit(solution)/shard_map/pallas_call | solution.py:510
